TPU v7x, 32 devices: a whole 2x2x4 slice. The times are simulated.
32 devices in a mesh: freq: 8 (over y, x, core), mode: 4 (over z).
Axes of the slice: x: 2, y: 2, z: 4, core: 2. Of those that a mesh axis runs over, the one named last changes fastest.
Arguments:
- excitation: bfloat16 [16, 2, 256, 2048], P(None, None, 'freq', 'mode'), may hold values from -6 to 6
- coupling: bfloat16 [3, 8, 2, 2048, 2048], P(None, 'freq', None, 'mode'), may hold values from -3 to 3, as said below
- wavenumber: float32 [256, 2048], P('freq', 'mode'), may hold values from 0.02 to 0.2
- mode_counts: int32 [256], P('freq'), may hold values from 128 to 2048, as said below
- seg_steps: int32 [3], replicated, may hold values from 8 to 64
- shapes: bfloat16 [8, 2048, 512], P('freq'), may hold values from -0.125 to 0.125
- spectrum: float32 [2, 256], P(None, 'freq'), may hold values from -6 to 6
Outputs:
- traces: float32 [16, 512, 4096], P('mode', 'freq')
Inputs may be any that keep to these rules, and one draw needn't show every extreme that they name: `mode_counts`: each count is a multiple of 128; counts tend to rise with frequency; the first frequency has 128 modes and the last has all 2048. `coupling`: the real part of each matrix is near the identity on its diagonal; all entries are independent otherwise.
All inputs are finite; a program needn't handle non-finite values.
Results may differ from a plain program's by a relative error of at most 0.015.
Values may be sent and summed in bfloat16 or wider, within the bound.
A program may use at most 128 MiB of HBM per device.

v0:
```python
import math

import jax
import jax.numpy as jnp
from jax import lax
from jax.sharding import PartitionSpec as P

NT = 4096


def make_table(count, offset_bin):
    freq_index = jnp.arange(count, dtype=jnp.int32)
    sample = jnp.arange(NT, dtype=jnp.int32)
    phase_step = (freq_index[:, None] + offset_bin) * sample[None, :] % NT
    angles = phase_step.astype(jnp.float32) * (2.0 * math.pi / NT)
    return jnp.stack([jnp.cos(angles), -jnp.sin(angles)], axis=0).astype(jnp.bfloat16)


def shards(excitation, coupling, wavenumber, mode_counts, seg_steps, shapes, spectrum):
    sources, _, bins_here, modes_here = excitation.shape
    all_modes = coupling.shape[-1]
    receivers = shapes.shape[-1]
    columns = sources * 2 * bins_here
    first_mode = lax.axis_index("mode") * modes_here
    mode_number = first_mode + jnp.arange(modes_here, dtype=jnp.int32)
    living = (mode_number[None, :] < mode_counts[:, None]).astype(jnp.float32)
    amplitude = (
        (excitation.astype(jnp.float32) * living).astype(jnp.bfloat16).reshape(columns, modes_here)
    )
    for segment in range(coupling.shape[0]):
        stacked = coupling[segment, 0].reshape(2 * modes_here, all_modes)

        def add_portion(running, portion, offset, stacked=stacked):
            return lax.dot_general(
                portion, stacked, (((1,), (1,)), ((), ())), preferred_element_type=jnp.float32
            )

        product = add_portion(
            jnp.zeros((columns, 2 * modes_here), jnp.float32),
            lax.all_gather(amplitude, "mode", axis=1, tiled=True),
            jnp.int32(0),
        )
        product = product.reshape(sources, 2, bins_here, 2, modes_here)
        coupled_real = product[:, 0, :, 0] - product[:, 1, :, 1]
        coupled_imaginary = product[:, 1, :, 0] + product[:, 0, :, 1]
        angles = wavenumber * seg_steps[segment].astype(jnp.float32)
        factor_real = living * jnp.cos(angles)
        factor_imaginary = living * jnp.sin(angles)
        amplitude = jnp.stack(
            [
                coupled_real * factor_real - coupled_imaginary * factor_imaginary,
                coupled_real * factor_imaginary + coupled_imaginary * factor_real,
            ],
            axis=1,
        )
        amplitude = amplitude.astype(jnp.bfloat16).reshape(columns, modes_here)
    mode_shapes = shapes[0]
    sources_here = sources // lax.axis_size("mode")
    local_shapes = lax.dynamic_slice_in_dim(mode_shapes, first_mode, modes_here, 0)
    field = lax.psum_scatter(
        jnp.dot(amplitude, local_shapes, preferred_element_type=jnp.float32),
        "mode",
        scatter_dimension=0,
        tiled=True,
    )
    field = field.reshape(sources_here, 2, bins_here, receivers)
    weight_real = spectrum[0][None, :, None]
    weight_imaginary = spectrum[1][None, :, None]
    weighted = jnp.stack(
        [
            weight_real * field[:, 0] - weight_imaginary * field[:, 1],
            weight_real * field[:, 1] + weight_imaginary * field[:, 0],
        ],
        axis=1,
    ).astype(jnp.bfloat16)
    all_bins = bins_here * lax.axis_size("freq")
    offset_bin = all_bins // 16
    table = make_table(all_bins, offset_bin)
    summed = lax.dot_general(
        lax.all_to_all(weighted, "freq", split_axis=3, concat_axis=2, tiled=True),
        table,
        (((1, 2), (0, 1)), ((), ())),
        preferred_element_type=jnp.float32,
    )
    return summed * (1.0 / math.sqrt(all_bins))


def solution(mesh):
    in_specs = (
        P(None, None, "freq", "mode"),
        P(None, "freq", None, "mode", None),
        P("freq", "mode"),
        P("freq"),
        P(),
        P("freq", None, None),
        P(None, "freq"),
    )
    out_specs = P("mode", "freq", None)
    return jax.shard_map(shards, mesh=mesh, in_specs=in_specs, out_specs=out_specs, check_vma=False)
```

profile of v0, /device:TPU:17, one launch (start us, length us, event | category | flops | bytes accessed | tf_op | source)
XLA Modules:
  0.0 364.0 jit_solution(14905670017927090053)
XLA Ops:
  6.5 0.0 copy-start
  6.5 0.0 all-gather.4.cloned.1.call-start
  6.5 0.9 compare_convert_fusion
  7.4 2.5 multiply_convert_fusion
  9.9 0.0 all-gather.4.cloned.1.call-update
  9.9 0.0 all-gather.6.cloned.1.call-start
  10.0 1.4 fusion.32
  13.3 1.6 compare_select_fusion.5
  14.8 75.6 %all-gather.4.cloned.1.call-done = bf16[1024,2048]{1,0:T(8,128)(2,1)} async-done(((bf16[1024,512]{1,0:T(8,128)(2,1)}), bf16[1024,2048]{1,0:T(8,128)(2,1)}) %all-gather.4.cloned.1.call-update) | async-done | bytes 4194320 | tf_op jit(solution)/shard_map/all_gather | solution.py:40
  90.4 7.6 %fusion.10 = f32[16,2,32,2,512]{4,2,3,1,0:T(8,128)S(1)} fusion(bf16[16,2,32,2048,1]{3,2,4,1,0:T(8,128)(2,1)} %bitcast.169, bf16[3,1,2,512,2048]{4,3,2,1,0:T(8,128)(2,1)} %param.8), kind=kOutput, calls=%fused_computation.15 | convolution fusion | flops 4294967296 | bytes 12582912 | tf_op jit(solution)/shard_map/dot_general | solution.py:34
  98.0 0.6 subtract_convert_fusion.2
  98.6 0.1 pad_maximum_fusion
  98.7 1.0 copy.52
  99.8 0.0 all-gather.6.cloned.1.call-update
  99.8 0.0 all-gather.8.cloned.1.call-start
  99.8 79.4 %all-gather.6.cloned.1.call-done = bf16[1024,2048]{1,0:T(8,128)(2,1)} async-done(((bf16[1024,512]{1,0:T(8,128)(2,1)}), bf16[1024,2048]{1,0:T(8,128)(2,1)}) %all-gather.6.cloned.1.call-update) | async-done | bytes 4194320 | tf_op jit(solution)/shard_map/all_gather | solution.py:40
  179.2 7.6 %fusion.8 = f32[16,2,32,2,512]{4,2,3,1,0:T(8,128)S(1)} fusion(bf16[16,2,32,2048,1]{3,2,4,1,0:T(8,128)(2,1)} %bitcast.171, bf16[3,1,2,512,2048]{4,3,2,1,0:T(8,128)(2,1)} %param.8), kind=kOutput, calls=%fused_computation.13 | convolution fusion | flops 4294967296 | bytes 12582912 | tf_op jit(solution)/shard_map/dot_general | solution.py:34
  186.8 0.6 subtract_convert_fusion.1
  187.5 0.1 pad_maximum_fusion.1
  187.6 1.0 copy.55
  188.6 0.0 all-gather.8.cloned.1.call-update
  188.7 0.0 reduce-scatter.2.cloned.1.call-start
  188.7 79.4 %all-gather.8.cloned.1.call-done = bf16[1024,2048]{1,0:T(8,128)(2,1)} async-done(((bf16[1024,512]{1,0:T(8,128)(2,1)}), bf16[1024,2048]{1,0:T(8,128)(2,1)}) %all-gather.8.cloned.1.call-update) | async-done | bytes 4194320 | tf_op jit(solution)/shard_map/all_gather | solution.py:40
  268.1 7.6 %fusion.6 = f32[16,2,32,2,512]{4,2,3,1,0:T(8,128)S(1)} fusion(bf16[16,2,32,2048,1]{3,2,4,1,0:T(8,128)(2,1)} %bitcast.170, bf16[3,1,2,512,2048]{4,3,2,1,0:T(8,128)(2,1)} %param.8), kind=kOutput, calls=%fused_computation.11 | convolution fusion | flops 4294967296 | bytes 12582912 | tf_op jit(solution)/shard_map/dot_general | solution.py:34
  275.7 0.6 subtract_convert_fusion
  276.3 0.1 pad_maximum_fusion.2
  276.4 0.1 copy.58
  276.5 0.0 copy-start.1
  276.6 0.0 copy-done
  276.6 2.0 fusion.27
  278.6 0.0 reduce-scatter.2.cloned.1.call-update
  278.6 0.0 copy-done.1
  278.6 43.4 %reduce-scatter.2.cloned.1.call-done = f32[256,512]{1,0:T(8,128)} async-done(((f32[1024,512]{1,0:T(8,128)}), f32[256,512]{1,0:T(8,128)}) %reduce-scatter.2.cloned.1.call-update) | async-done | bytes 524304 | tf_op jit(solution)/shard_map/reduce_scatter | solution.py:60
  322.1 1.2 subtract_convert_fusion.3
  323.3 0.8 copy.59
  324.1 1.7 reshape.401
  325.7 4.3 %all-to-all-start = ((bf16[8,2,8192]{2,1,0:T(2,128)(2,1)}), bf16[8,2,8192]{2,1,0:T(2,128)(2,1)S(1)}, u32[]{:S(2)}, u32[]{:S(2)}) async-start(bf16[8,2,8192]{2,1,0:T(2,128)(2,1)} %reshape.401), calls=%async_computation.1 | async-start | bytes 524288 | tf_op jit(solution)/shard_map/all_to_all | solution.py:80
  330.0 18.9 %cosine_convert_fusion = (bf16[1,256,4096]{2,1,0:T(8,128)(2,1)}, bf16[1,256,4096]{2,1,0:T(8,128)(2,1)}) fusion(s32[256]{0:T(256)S(1)} %iota_add_fusion.1), kind=kLoop, calls=%fused_computation.18 | loop fusion | flops 17825792 | bytes 4195328 | tf_op jit(solution)/shard_map/convert
  348.9 0.0 all-to-all-done
  348.9 0.5 reshape.402
  349.4 2.4 copy.72
  351.8 5.7 %fusion = f32[4,64,4096]{2,1,0:T(8,128)} fusion(bf16[4,2,256,64]{3,2,1,0:T(8,128)(2,1)} %bitcast.167, bf16[1,256,4096]{2,1,0:T(8,128)(2,1)} %get-tuple-element.20, bf16[1,256,4096]{2,1,0:T(8,128)(2,1)} %get-tuple-element.19), kind=kOutput, calls=%fused_computation.4 | convolution fusion | flops 1076887552 | bytes 8650752 | tf_op jit(solution)/shard_map/dot_general | solution.py:79
  (4 shorter events, 0.0 us)
Async XLA Ops:
  6.5 270.0 %copy-start = (bf16[1,2048,512]{2,1,0:T(8,128)(2,1)S(1)}, bf16[1,2048,512]{2,1,0:T(8,128)(2,1)}, u32[]{:S(2)}) copy-start(bf16[1,2048,512]{2,1,0:T(8,128)(2,1)} %param.12) | copy-start | bytes 6291460
  6.5 83.9 %all-gather.4.cloned.1.call-start = ((), (), s32[]{:S(2)}) async-start(), calls=%async_computation.2 | async-start | bytes 5242880 | tf_op jit(solution)/shard_map/all_gather | solution.py:40
  9.9 169.3 %all-gather.6.cloned.1.call-start = ((), (), s32[]{:S(2)}) async-start(), calls=%async_computation.3 | async-start | bytes 5242880 | tf_op jit(solution)/shard_map/all_gather | solution.py:40
  99.8 168.3 %all-gather.8.cloned.1.call-start = ((), (), s32[]{:S(2)}) async-start(), calls=%async_computation.4 | async-start | bytes 5242880 | tf_op jit(solution)/shard_map/all_gather | solution.py:40
  188.7 133.4 %reduce-scatter.2.cloned.1.call-start = ((), (), s32[]{:S(2)}) async-start(), calls=%async_computation.5 | async-start | bytes 2621440 | tf_op jit(solution)/shard_map/reduce_scatter | solution.py:60
  276.5 2.1 copy-start.1
  325.7 23.2 %all-to-all-start = ((bf16[8,2,8192]{2,1,0:T(2,128)(2,1)}), bf16[8,2,8192]{2,1,0:T(2,128)(2,1)S(1)}, u32[]{:S(2)}, u32[]{:S(2)}) async-start(bf16[8,2,8192]{2,1,0:T(2,128)(2,1)} %reshape.401), calls=%async_computation.1 | async-start | bytes 524288 | tf_op jit(solution)/shard_map/all_to_all | solution.py:80
Sparse Core Ops, SparseCore 0:
  10.0 80.3 all-gather.3
  99.9 79.2 all-gather.5
  188.8 79.2 all-gather.7
  278.7 43.2 reduce-scatter.1
where the time goes:
time: 366 us; the launch traced here: 364 us
  waiting for transfers between devices  278 us (76%)
  matrix products  30.5 us (8%)
  other arithmetic  27.2 us (7%)
  between operations  15.2 us (4%)
  local copies, waits for them, and re-layouts  8.93 us (2%)
  starting transfers between devices  4.39 us (1%)
    all_gather x3, waiting for transfers between devices, shards(): lax.all_gather(amplitude, 'mode', axis=1, tiled=True)  234 us
    reduce_scatter x1, waiting for transfers between devices, shards(): lax.psum_scatter(jnp.dot(amplitude, local_shapes, preferred_element_type=...  43.4 us
    dot_general x3, matrix products, add_portion(): lax.dot_general(portion, stacked, (((1,), (1,)), ((), ())), preferred_ele...  22.8 us
    another operation x5, other arithmetic  21.9 us
  transfers between devices with their start and end apart: 5, of which 4 were waited for; matrix products, arithmetic and copies ran while one was open for 6% of the time, Pallas kernels for 0%

commit v1 on v0

v1 whole, which is shorter than its diff:
```python
import functools
import math

import jax
import jax.numpy as jnp
from jax import lax
from jax.experimental import pallas as pl
from jax.experimental.pallas import tpu as pltpu
from jax.sharding import PartitionSpec as P

NT = 4096
LANES = 128


def propagate(
    n, nf, offset_bin, exc, coupling, wavenumber, counts, steps, shapes, weights,
    table, received,
    matrix, amp, factor, weighted, landed,
    load_sem, send_sem, recv_sem, own_send, own_recv, out_send, out_recv,
):
    segments = coupling.shape[0]
    sources, _, bins, modes = exc.shape
    cs = sources // n
    half = cs * bins
    receivers = shapes.shape[-1]
    rh = receivers // nf
    phases = segments * n
    me = lax.axis_index("mode")
    band = lax.axis_index("freq")

    def load(g):
        return pltpu.make_async_copy(coupling.at[g, 0], matrix.at[g], load_sem.at[g])

    def hop(g, k, sign, d):
        shard = me - sign * d
        way = (sign + 1) // 2
        return pltpu.make_async_remote_copy(
            src_ref=amp.at[g, k, shard],
            dst_ref=amp.at[g, k, shard],
            send_sem=send_sem.at[g, k, way, d],
            recv_sem=recv_sem.at[g, k, way, d],
            device_id={"mode": me + sign},
            device_id_type=pl.DeviceIdType.MESH,
        )

    def arrival(g, k, sign, d):
        shard = me - sign * (d + 1)
        way = (sign + 1) // 2
        return pltpu.make_async_remote_copy(
            src_ref=amp.at[g, k, shard],
            dst_ref=amp.at[g, k, shard],
            send_sem=send_sem.at[g, k, way, d],
            recv_sem=recv_sem.at[g, k, way, d],
            device_id={"mode": me - sign},
            device_id_type=pl.DeviceIdType.MESH,
        )

    def inside(z):
        return jnp.logical_and(z >= 0, z < n)

    lead = jnp.where(me < n // 2, -1, 1)

    def send_own(g, k):
        for sign in (lead, -lead):
            @pl.when(inside(me + sign))
            def _(sign=sign):
                hop(g, k, sign, 0).start()

    def to_owner(k):
        return pltpu.make_async_remote_copy(
            src_ref=amp.at[segments, k, me],
            dst_ref=amp.at[segments, k, me],
            send_sem=own_send.at[k],
            recv_sem=own_recv.at[me],
            device_id={"mode": k},
            device_id_type=pl.DeviceIdType.MESH,
        )

    for g in range(segments):
        load(g).start()

    barrier = pltpu.get_barrier_semaphore()

    @pl.loop(1, n)
    def _(i):
        pl.semaphore_signal(
            barrier, inc=1, device_id={"mode": lax.rem(me + i, n)},
            device_id_type=pl.DeviceIdType.MESH,
        )

    @pl.loop(1, nf)
    def _(i):
        pl.semaphore_signal(
            barrier, inc=1, device_id={"freq": lax.rem(band + i, nf)},
            device_id_type=pl.DeviceIdType.MESH,
        )

    mode_number = me * modes + lax.broadcasted_iota(jnp.int32, (bins, modes), 1)
    living = jnp.where(mode_number < counts[...], 1.0, 0.0).astype(jnp.float32)

    @pl.loop(0, n)
    def _(k):
        for c in range(2):
            x = exc[pl.ds(k * cs, cs), c].astype(jnp.float32) * living[None]
            amp[0, k, me, c * half:(c + 1) * half, :] = (
                x.reshape(half, modes).astype(jnp.bfloat16)
            )

    pl.semaphore_wait(barrier, n - 1 + nf - 1)
    send_own(0, 0)
    if n > 1:
        send_own(0, 1)

    for g in range(segments):
        angle = wavenumber[...] * steps[g].astype(jnp.float32)
        factor[g, 0] = living * jnp.cos(angle)
        factor[g, 1] = living * jnp.sin(angle)

    def table_block(j):
        f = j * bins + offset_bin + lax.broadcasted_iota(jnp.int32, (bins, LANES), 0)
        lane = lax.broadcasted_iota(jnp.int32, (bins, LANES), 1)
        unit = 2.0 * math.pi / NT
        fine = lax.rem(f * lane, NT).astype(jnp.float32) * unit
        coarse = lax.rem(f * (lane * LANES), NT).astype(jnp.float32) * unit
        cos_fine, sin_fine = jnp.cos(fine), jnp.sin(fine)
        cos_coarse, sin_coarse = jnp.cos(coarse), jnp.sin(coarse)
        row = pl.multiple_of(j * (2 * bins), 2 * bins)
        for a in range(NT // LANES):
            ca = cos_coarse[:, a:a + 1]
            sa = sin_coarse[:, a:a + 1]
            at = slice(a * LANES, (a + 1) * LANES)
            table[pl.ds(row, bins), at] = (ca * cos_fine - sa * sin_fine).astype(jnp.bfloat16)
            table[pl.ds(row + bins, bins), at] = (
                -(sa * cos_fine + ca * sin_fine)
            ).astype(jnp.bfloat16)

    width = min(256, modes)

    @pl.loop(0, phases)
    def _(p):
        g = p // n
        k = lax.rem(p, n)

        @pl.when(jnp.logical_and(g == 0, k + 2 < n))
        def _():
            send_own(0, k + 2)

        for d in range(n - 1):
            for sign in (lead, -lead):
                @pl.when(inside(me - sign * (d + 1)))
                def _(sign=sign, d=d):
                    arrival(g, k, sign, d).wait_recv()
                    if d + 1 < n - 1:
                        @pl.when(inside(me + sign))
                        def _():
                            hop(g, k, sign, d + 1).start()

        @pl.when(k == 0)
        def _():
            load(g).wait()

        @pl.loop(0, modes // width)
        def _(tile):
            rows = pl.ds(pl.multiple_of(tile * width, width), width)
            by_real = jnp.zeros((2 * half, width), jnp.float32)
            by_imag = jnp.zeros((2 * half, width), jnp.float32)
            for z in range(n):
                a = amp[g, k, z]
                cols = slice(z * modes, (z + 1) * modes)
                dims = (((1,), (1,)), ((), ()))
                by_real += lax.dot_general(
                    a, matrix[g, 0, rows, cols], dims, preferred_element_type=jnp.float32
                )
                by_imag += lax.dot_general(
                    a, matrix[g, 1, rows, cols], dims, preferred_element_type=jnp.float32
                )
            real = (by_real[:half] - by_imag[half:]).reshape(cs, bins, width)
            imag = (by_real[half:] + by_imag[:half]).reshape(cs, bins, width)
            fr = factor[g, 0, :, rows][None]
            fi = factor[g, 1, :, rows][None]
            amp[g + 1, k, me, 0:half, rows] = (
                (real * fr - imag * fi).reshape(half, width).astype(jnp.bfloat16)
            )
            amp[g + 1, k, me, half:2 * half, rows] = (
                (real * fi + imag * fr).reshape(half, width).astype(jnp.bfloat16)
            )

        @pl.when(g + 1 < segments)
        def _():
            send_own(g + 1, k)

        @pl.when(jnp.logical_and(g + 1 == segments, k != me))
        def _():
            to_owner(k).start()

        @pl.loop(0, (nf - p + phases - 1) // phases)
        def _(i):
            table_block(p + i * phases)

    @pl.loop(1, n)
    def _(i):
        z = lax.rem(me + i, n)
        pltpu.make_async_remote_copy(
            src_ref=amp.at[segments, me, z],
            dst_ref=amp.at[segments, me, z],
            send_sem=own_send.at[z],
            recv_sem=own_recv.at[z],
            device_id={"mode": z},
            device_id_type=pl.DeviceIdType.MESH,
        ).wait_recv()

    field = jnp.zeros((2 * half, receivers), jnp.float32)
    for z in range(n):
        field += jnp.dot(
            amp[segments, me, z], shapes[0, z * modes:(z + 1) * modes, :],
            preferred_element_type=jnp.float32,
        )
    wr, wi = weights[:, 0:1], weights[:, 1:2]
    fr, fi = field[:half], field[half:]
    weighted[0] = (wr * fr - wi * fi).T.astype(jnp.bfloat16)
    weighted[1] = (wr * fi + wi * fr).T.astype(jnp.bfloat16)

    def to_receiver(j, slot):
        return pltpu.make_async_remote_copy(
            src_ref=weighted.at[:, pl.ds(pl.multiple_of(j * rh, rh), rh)],
            dst_ref=landed.at[slot],
            send_sem=out_send.at[j],
            recv_sem=out_recv.at[slot],
            device_id={"freq": j},
            device_id_type=pl.DeviceIdType.MESH,
        )

    @pl.loop(1, nf)
    def _(i):
        to_receiver(lax.rem(band + i, nf), band).start()

    received[band] = weighted[:, pl.ds(pl.multiple_of(band * rh, rh), rh), :]

    @pl.loop(1, nf)
    def _(i):
        j = lax.rem(band + i, nf)
        to_receiver(j, j).wait_recv()
        received[j] = landed[j]

    @pl.loop(1, nf)
    def _(i):
        to_receiver(lax.rem(band + i, nf), band).wait_send()

    @pl.loop(0, phases)
    def _(p):
        g = p // n
        k = lax.rem(p, n)
        for d in range(n - 1):
            for sign in (lead, -lead):
                @pl.when(jnp.logical_and(inside(me - sign * d), inside(me + sign)))
                def _(sign=sign, d=d):
                    hop(g, k, sign, d).wait_send()

    @pl.loop(1, n)
    def _(i):
        to_owner(lax.rem(me + i, n)).wait_send()


def shards(excitation, coupling, wavenumber, mode_counts, seg_steps, shapes, spectrum):
    n = lax.axis_size("mode")
    nf = lax.axis_size("freq")
    sources, _, bins, modes = excitation.shape
    segments, _, _, _, all_modes = coupling.shape
    receivers = shapes.shape[-1]
    cs = sources // n
    half = cs * bins
    rh = receivers // nf
    all_bins = bins * nf
    vmem = pl.BlockSpec(memory_space=pltpu.VMEM)
    dma = pltpu.SemaphoreType.DMA
    table, received = pl.pallas_call(
        functools.partial(propagate, n, nf, all_bins // 16),
        out_shape=(
            jax.ShapeDtypeStruct((nf * 2 * bins, NT), jnp.bfloat16),
            jax.ShapeDtypeStruct((nf, 2, rh, half), jnp.bfloat16),
        ),
        in_specs=[
            vmem, pl.BlockSpec(memory_space=pl.ANY), vmem, vmem,
            pl.BlockSpec(memory_space=pltpu.SMEM), vmem, vmem,
        ],
        out_specs=(vmem, vmem),
        scratch_shapes=[
            pltpu.VMEM((segments, 2, modes, all_modes), jnp.bfloat16),
            pltpu.VMEM((segments + 1, n, n, 2 * half, modes), jnp.bfloat16),
            pltpu.VMEM((segments, 2, bins, modes), jnp.float32),
            pltpu.VMEM((2, receivers, half), jnp.bfloat16),
            pltpu.VMEM((nf, 2, rh, half), jnp.bfloat16),
            dma((segments,)),
            dma((segments, n, 2, n - 1)),
            dma((segments, n, 2, n - 1)),
            dma((n,)),
            dma((n,)),
            dma((nf,)),
            dma((nf,)),
        ],
        compiler_params=pltpu.CompilerParams(
            collective_id=0, has_side_effects=True, vmem_limit_bytes=60 * 1024 * 1024
        ),
        name="propagate",
    )(
        excitation, coupling, wavenumber, mode_counts.reshape(bins, 1), seg_steps, shapes,
        jnp.tile(spectrum.T, (cs, 1)),
    )
    left = received.reshape(nf, 2, rh, cs, bins).transpose(3, 2, 0, 1, 4)
    left = left.reshape(cs, rh, nf * 2 * bins)
    summed = lax.dot_general(
        left, table, (((2,), (0,)), ((), ())), preferred_element_type=jnp.float32
    )
    return summed * (1.0 / math.sqrt(all_bins))


def solution(mesh):
    in_specs = (
        P(None, None, "freq", "mode"),
        P(None, "freq", None, "mode", None),
        P("freq", "mode"),
        P("freq"),
        P(),
        P("freq", None, None),
        P(None, "freq"),
    )
    out_specs = P("mode", "freq", None)
    return jax.shard_map(shards, mesh=mesh, in_specs=in_specs, out_specs=out_specs, check_vma=False)
```

time: 366 us -> 254 us (0.69)
  the two profiles are of different devices: /device:TPU:17 before, /device:TPU:25 now
where the time goes in v1:
time: 254 us; the launch traced here: 253 us
  Pallas kernels  244 us (96%)
  matrix products  5.51 us (2%)
  local copies, waits for them, and re-layouts  4.01 us (2%)
    pallas_call x1, Pallas kernels, shards(): pl.pallas_call(functools.partial(propagate, n, nf, all_bins // 16), out_s...  244 us
    dot_general x1, matrix products, shards(): lax.dot_general(left, table, (((2,), (0,)), ((), ())), preferred_element_...  5.51 us

profile of v1, /device:TPU:25, one launch (start us, length us, event | category | flops | bytes accessed | tf_op | source)
XLA Modules:
  0.0 253.4 jit_solution(14144417713679033099)
XLA Ops:
  0.0 1.3 copy.12.counts
  1.3 0.8 copy.11
  2.1 0.6 tile.4
  2.7 243.8 %propagate.1 = (bf16[512,4096]{1,0:T(8,128)(2,1)}, bf16[8,2,64,128]{3,2,1,0:T(8,128)(2,1)}) custom-call(bf16[16,2,32,512]{3,2,1,0:T(8,128)(2,1)} %exc.1, bf16[3,1,2,512,2048]{4,3,2,1,0:T(8,128)(2,1)} %coupling.1, f32[32,512]{1,0:T(8,128)} %wavenumber.1, s32[32,1]{1,0:T(8,128)} %copy.12.counts, s32[3]{0:T(128)} %steps.1, bf16[1,2048,512]{2,1,0:T(8,128)(2,1)} %shapes.1, ...), custom_call_target="tpu_custom_call" | custom-call | tf_op jit(solution)/shard_map/propagate/pallas_call | solution.py:276
  246.6 1.2 copy.13
  247.8 0.1 copy.14
  247.9 5.5 %convolution_multiply_fusion = f32[4,64,4096]{2,1,0:T(8,128)} fusion(bf16[4,64,512]{1,2,0:T(8,128)(2,1)S(1)} %bitcast.11, bf16[512,4096]{1,0:T(8,128)(2,1)} %get-tuple-element.8), kind=kOutput, calls=%fused_computation | convolution fusion | flops 1074790400 | bytes 8650752 | tf_op jit(solution)/shard_map/dot_general | solution.py:311

commit v2 on v1

--- a/solution.py
+++ b/solution.py
@@ -12,11 +12,17 @@
 LANES = 128
 
 
+def phase_order(segments, n):
+    pairs = [(g, position) for g in range(segments) for position in range(n)]
+    return sorted(pairs, key=lambda pair: (pair[1] + pair[0] * 0.625 * n, pair[0]))
+
+
 def propagate(
     n, nf, offset_bin, exc, coupling, wavenumber, counts, steps, shapes, weights,
     table, received,
-    matrix, amp, factor, weighted, landed,
+    matrix, amp, factor, weighted, landed, lent, lent_factor,
     load_sem, send_sem, recv_sem, own_send, own_recv, out_send, out_recv,
+    lend_send, lend_recv, lend_factor_sem,
 ):
     segments = coupling.shape[0]
     sources, _, bins, modes = exc.shape
@@ -28,6 +34,55 @@
     me = lax.axis_index("mode")
     band = lax.axis_index("freq")
 
+    relieve = n >= 4 and segments >= 2
+    last = segments - 1
+    order = phase_order(segments, n)
+    first_last = [g for g, _ in order].index(last)
+    lending = max(first_last - 1, 1)
+    pieces = max(last, 1) * n
+    piece = modes // pieces
+
+    def at_end(z):
+        return jnp.logical_and(relieve, jnp.logical_or(z == 0, z == n - 1))
+
+    edge = at_end(me)
+    helper = jnp.logical_and(relieve, jnp.logical_or(me == 1, me == n - 2))
+    partner = jnp.where(me == 1, 0, n - 1)
+    inward = jnp.where(me == 0, min(1, n - 1), max(n - 2, 0))
+
+    def owner(position):
+        return jnp.where(
+            lax.rem(position, 2) == 0, position // 2, n - 1 - position // 2
+        )
+
+    def phase(p):
+        g, position = jnp.int32(0), jnp.int32(0)
+        for i, (at_g, at_position) in enumerate(order):
+            g = jnp.where(p == i, at_g, g)
+            position = jnp.where(p == i, at_position, position)
+        return g, position
+
+    def lend(q):
+        rows = pl.ds(pl.multiple_of(q * piece, piece), piece)
+        return pltpu.make_async_remote_copy(
+            src_ref=matrix.at[last, :, rows],
+            dst_ref=lent.at[:, rows],
+            send_sem=lend_send.at[q],
+            recv_sem=lend_recv.at[q],
+            device_id={"mode": inward},
+            device_id_type=pl.DeviceIdType.MESH,
+        )
+
+    def lend_factor():
+        return pltpu.make_async_remote_copy(
+            src_ref=factor.at[last],
+            dst_ref=lent_factor,
+            send_sem=lend_factor_sem.at[0],
+            recv_sem=lend_factor_sem.at[1],
+            device_id={"mode": inward},
+            device_id_type=pl.DeviceIdType.MESH,
+        )
+
     def load(g):
         return pltpu.make_async_copy(coupling.at[g, 0], matrix.at[g], load_sem.at[g])
 
@@ -60,18 +115,21 @@
 
     lead = jnp.where(me < n // 2, -1, 1)
 
+    def wanted(g, z):
+        return jnp.logical_and(inside(z), jnp.logical_not(jnp.logical_and(g == last, at_end(z))))
+
     def send_own(g, k):
         for sign in (lead, -lead):
-            @pl.when(inside(me + sign))
+            @pl.when(wanted(g, me + sign))
             def _(sign=sign):
                 hop(g, k, sign, 0).start()
 
-    def to_owner(k):
-        return pltpu.make_async_remote_copy(
-            src_ref=amp.at[segments, k, me],
-            dst_ref=amp.at[segments, k, me],
-            send_sem=own_send.at[k],
-            recv_sem=own_recv.at[me],
+    def to_owner(k, shard, which):
+        return pltpu.make_async_remote_copy(
+            src_ref=amp.at[segments, k, shard],
+            dst_ref=amp.at[segments, k, shard],
+            send_sem=own_send.at[k, which],
+            recv_sem=own_recv.at[shard],
             device_id={"mode": k},
             device_id_type=pl.DeviceIdType.MESH,
         )
@@ -107,14 +165,19 @@
             )
 
     pl.semaphore_wait(barrier, n - 1 + nf - 1)
-    send_own(0, 0)
+    send_own(0, owner(jnp.int32(0)))
     if n > 1:
-        send_own(0, 1)
+        send_own(0, owner(jnp.int32(1)))
 
     for g in range(segments):
         angle = wavenumber[...] * steps[g].astype(jnp.float32)
         factor[g, 0] = living * jnp.cos(angle)
         factor[g, 1] = living * jnp.sin(angle)
+
+    @pl.when(edge)
+    def _():
+        lend_factor().start()
+        load(last).wait()
 
     def table_block(j):
         f = j * bins + offset_bin + lax.broadcasted_iota(jnp.int32, (bins, LANES), 0)
@@ -136,29 +199,7 @@
 
     width = min(256, modes)
 
-    @pl.loop(0, phases)
-    def _(p):
-        g = p // n
-        k = lax.rem(p, n)
-
-        @pl.when(jnp.logical_and(g == 0, k + 2 < n))
-        def _():
-            send_own(0, k + 2)
-
-        for d in range(n - 1):
-            for sign in (lead, -lead):
-                @pl.when(inside(me - sign * (d + 1)))
-                def _(sign=sign, d=d):
-                    arrival(g, k, sign, d).wait_recv()
-                    if d + 1 < n - 1:
-                        @pl.when(inside(me + sign))
-                        def _():
-                            hop(g, k, sign, d + 1).start()
-
-        @pl.when(k == 0)
-        def _():
-            load(g).wait()
-
+    def couple(source, turn, g, k, shard):
         @pl.loop(0, modes // width)
         def _(tile):
             rows = pl.ds(pl.multiple_of(tile * width, width), width)
@@ -169,45 +210,105 @@
                 cols = slice(z * modes, (z + 1) * modes)
                 dims = (((1,), (1,)), ((), ()))
                 by_real += lax.dot_general(
-                    a, matrix[g, 0, rows, cols], dims, preferred_element_type=jnp.float32
+                    a, source[0, rows, cols], dims, preferred_element_type=jnp.float32
                 )
                 by_imag += lax.dot_general(
-                    a, matrix[g, 1, rows, cols], dims, preferred_element_type=jnp.float32
+                    a, source[1, rows, cols], dims, preferred_element_type=jnp.float32
                 )
             real = (by_real[:half] - by_imag[half:]).reshape(cs, bins, width)
             imag = (by_real[half:] + by_imag[:half]).reshape(cs, bins, width)
-            fr = factor[g, 0, :, rows][None]
-            fi = factor[g, 1, :, rows][None]
-            amp[g + 1, k, me, 0:half, rows] = (
+            fr = turn[0, :, rows][None]
+            fi = turn[1, :, rows][None]
+            amp[g + 1, k, shard, 0:half, rows] = (
                 (real * fr - imag * fi).reshape(half, width).astype(jnp.bfloat16)
             )
-            amp[g + 1, k, me, half:2 * half, rows] = (
+            amp[g + 1, k, shard, half:2 * half, rows] = (
                 (real * fi + imag * fr).reshape(half, width).astype(jnp.bfloat16)
             )
 
-        @pl.when(g + 1 < segments)
+    @pl.loop(0, phases)
+    def _(p):
+        g, position = phase(p)
+        k = owner(position)
+        active = wanted(g, me)
+        helping = jnp.logical_and(g == last, helper)
+
+        @pl.when(jnp.logical_and(g == 0, position + 2 < n))
+        def _():
+            send_own(0, owner(position + 2))
+
+        if relieve:
+            @pl.when(jnp.logical_and(edge, p < lending))
+            def _():
+                @pl.loop(p * pieces // lending, (p + 1) * pieces // lending)
+                def _(q):
+                    lend(q).start()
+
+        for d in range(n - 1):
+            for sign in (lead, -lead):
+                @pl.when(jnp.logical_and(active, inside(me - sign * (d + 1))))
+                def _(sign=sign, d=d):
+                    arrival(g, k, sign, d).wait_recv()
+                    if d + 1 < n - 1:
+                        @pl.when(wanted(g, me + sign))
+                        def _():
+                            hop(g, k, sign, d + 1).start()
+
+        @pl.when(jnp.logical_and(position == 0, active))
+        def _():
+            load(g).wait()
+
+        @pl.when(active)
+        def _():
+            couple(matrix.at[g], factor.at[g], g, k, me)
+
+        @pl.when(g < last)
         def _():
             send_own(g + 1, k)
 
-        @pl.when(jnp.logical_and(g + 1 == segments, k != me))
-        def _():
-            to_owner(k).start()
+        @pl.when(jnp.logical_and(jnp.logical_and(g == last, active), k != me))
+        def _():
+            to_owner(k, me, 0).start()
+
+        if relieve:
+            @pl.when(helping)
+            def _():
+                @pl.when(position == 0)
+                def _():
+                    lend_factor().wait_recv()
+
+                    @pl.loop(0, pieces)
+                    def _(q):
+                        lend(q).wait_recv()
+
+                couple(lent, lent_factor, last, k, partner)
+
+                @pl.when(k != me)
+                def _():
+                    to_owner(k, partner, 1).start()
 
         @pl.loop(0, (nf - p + phases - 1) // phases)
         def _(i):
             table_block(p + i * phases)
 
-    @pl.loop(1, n)
-    def _(i):
-        z = lax.rem(me + i, n)
-        pltpu.make_async_remote_copy(
-            src_ref=amp.at[segments, me, z],
-            dst_ref=amp.at[segments, me, z],
-            send_sem=own_send.at[z],
-            recv_sem=own_recv.at[z],
-            device_id={"mode": z},
-            device_id_type=pl.DeviceIdType.MESH,
-        ).wait_recv()
+    @pl.loop(0, n)
+    def _(z):
+        here = jnp.logical_or(
+            jnp.logical_and(z == me, jnp.logical_not(edge)),
+            jnp.logical_and(helper, z == partner),
+        )
+
+        @pl.when(jnp.logical_not(here))
+        def _():
+            sender = jnp.where(at_end(z), jnp.where(z == 0, 1, n - 2), z)
+            pltpu.make_async_remote_copy(
+                src_ref=amp.at[segments, me, z],
+                dst_ref=amp.at[segments, me, z],
+                send_sem=own_send.at[me, 0],
+                recv_sem=own_recv.at[z],
+                device_id={"mode": sender},
+                device_id_type=pl.DeviceIdType.MESH,
+            ).wait_recv()
 
     field = jnp.zeros((2 * half, receivers), jnp.float32)
     for z in range(n):
@@ -252,13 +353,31 @@
         k = lax.rem(p, n)
         for d in range(n - 1):
             for sign in (lead, -lead):
-                @pl.when(jnp.logical_and(inside(me - sign * d), inside(me + sign)))
+                @pl.when(jnp.logical_and(inside(me - sign * d), wanted(g, me + sign)))
                 def _(sign=sign, d=d):
                     hop(g, k, sign, d).wait_send()
 
     @pl.loop(1, n)
     def _(i):
-        to_owner(lax.rem(me + i, n)).wait_send()
+        k = lax.rem(me + i, n)
+
+        @pl.when(jnp.logical_not(edge))
+        def _():
+            to_owner(k, me, 0).wait_send()
+
+        if relieve:
+            @pl.when(helper)
+            def _():
+                to_owner(k, partner, 1).wait_send()
+
+    if relieve:
+        @pl.when(edge)
+        def _():
+            lend_factor().wait_send()
+
+            @pl.loop(0, pieces)
+            def _(q):
+                lend(q).wait_send()
 
 
 def shards(excitation, coupling, wavenumber, mode_counts, seg_steps, shapes, spectrum):
@@ -290,13 +409,18 @@
             pltpu.VMEM((segments, 2, bins, modes), jnp.float32),
             pltpu.VMEM((2, receivers, half), jnp.bfloat16),
             pltpu.VMEM((nf, 2, rh, half), jnp.bfloat16),
+            pltpu.VMEM((2, modes, all_modes), jnp.bfloat16),
+            pltpu.VMEM((2, bins, modes), jnp.float32),
             dma((segments,)),
             dma((segments, n, 2, n - 1)),
             dma((segments, n, 2, n - 1)),
-            dma((n,)),
+            dma((n, 2)),
             dma((n,)),
             dma((nf,)),
             dma((nf,)),
+            dma((max(segments - 1, 1) * n,)),
+            dma((max(segments - 1, 1) * n,)),
+            dma((2,)),
         ],
         compiler_params=pltpu.CompilerParams(
             collective_id=0, has_side_effects=True, vmem_limit_bytes=60 * 1024 * 1024

time: 254 us -> 238 us (0.937)
  the two profiles are of different devices: /device:TPU:25 before, /device:TPU:17 now
where the time goes in v2:
time: 238 us
  Pallas kernels  229 us (96%)
  matrix products  5.51 us (2%)
  local copies, waits for them, and re-layouts  4.01 us (2%)
    pallas_call x1, Pallas kernels, shards(): pl.pallas_call(functools.partial(propagate, n, nf, all_bins // 16), out_s...  229 us
    dot_general x1, matrix products, shards(): lax.dot_general(left, table, (((2,), (0,)), ((), ())), preferred_element_...  5.51 us

profile of v2, /device:TPU:17, one launch (start us, length us, event | category | flops | bytes accessed | tf_op | source)
XLA Modules:
  0.0 238.3 jit_solution(9563176426239654334)
XLA Ops:
  0.0 1.3 copy.12.counts
  1.3 0.8 copy.11
  2.1 0.6 tile.4
  2.7 228.7 %propagate.1 = (bf16[512,4096]{1,0:T(8,128)(2,1)}, bf16[8,2,64,128]{3,2,1,0:T(8,128)(2,1)}) custom-call(bf16[16,2,32,512]{3,2,1,0:T(8,128)(2,1)} %exc.1, bf16[3,1,2,512,2048]{4,3,2,1,0:T(8,128)(2,1)} %coupling.1, f32[32,512]{1,0:T(8,128)} %wavenumber.1, s32[32,1]{1,0:T(8,128)} %copy.12.counts, s32[3]{0:T(128)} %steps.1, bf16[1,2048,512]{2,1,0:T(8,128)(2,1)} %shapes.1, ...), custom_call_target="tpu_custom_call" | custom-call | tf_op jit(solution)/shard_map/propagate/pallas_call | solution.py:395
  231.5 1.2 copy.13
  232.7 0.1 copy.14
  232.8 5.5 %convolution_multiply_fusion = f32[4,64,4096]{2,1,0:T(8,128)} fusion(bf16[4,64,512]{1,2,0:T(8,128)(2,1)S(1)} %bitcast.11, bf16[512,4096]{1,0:T(8,128)(2,1)} %get-tuple-element.8), kind=kOutput, calls=%fused_computation | convolution fusion | flops 1074790400 | bytes 8650752 | tf_op jit(solution)/shard_map/dot_general | solution.py:435

commit v3 on v2

--- a/solution.py
+++ b/solution.py
@@ -199,32 +199,49 @@
 
     width = min(256, modes)
 
-    def couple(source, turn, g, k, shard):
-        @pl.loop(0, modes // width)
-        def _(tile):
-            rows = pl.ds(pl.multiple_of(tile * width, width), width)
-            by_real = jnp.zeros((2 * half, width), jnp.float32)
-            by_imag = jnp.zeros((2 * half, width), jnp.float32)
-            for z in range(n):
-                a = amp[g, k, z]
-                cols = slice(z * modes, (z + 1) * modes)
-                dims = (((1,), (1,)), ((), ()))
-                by_real += lax.dot_general(
-                    a, source[0, rows, cols], dims, preferred_element_type=jnp.float32
+    def forward(p, d):
+        g, position = phase(p)
+        k = owner(position)
+        for sign in (lead, -lead):
+            @pl.when(
+                jnp.logical_and(
+                    jnp.logical_and(p < phases, wanted(g, me)),
+                    jnp.logical_and(inside(me - sign * (d + 1)), wanted(g, me + sign)),
                 )
-                by_imag += lax.dot_general(
-                    a, source[1, rows, cols], dims, preferred_element_type=jnp.float32
-                )
-            real = (by_real[:half] - by_imag[half:]).reshape(cs, bins, width)
-            imag = (by_real[half:] + by_imag[:half]).reshape(cs, bins, width)
-            fr = turn[0, :, rows][None]
-            fi = turn[1, :, rows][None]
-            amp[g + 1, k, shard, 0:half, rows] = (
-                (real * fr - imag * fi).reshape(half, width).astype(jnp.bfloat16)
             )
-            amp[g + 1, k, shard, half:2 * half, rows] = (
-                (real * fi + imag * fr).reshape(half, width).astype(jnp.bfloat16)
+            def _(sign=sign):
+                arrival(g, k, sign, d).wait_recv()
+                hop(g, k, sign, d + 1).start()
+
+    tiles = modes // width
+
+    def couple(source, turn, g, k, shard, tile):
+        rows = slice(tile * width, (tile + 1) * width)
+        by_real = jnp.zeros((2 * half, width), jnp.float32)
+        by_imag = jnp.zeros((2 * half, width), jnp.float32)
+        for z in range(n):
+            a = amp[g, k, z]
+            cols = slice(z * modes, (z + 1) * modes)
+            dims = (((1,), (1,)), ((), ()))
+            by_real += lax.dot_general(
+                a, source[0, rows, cols], dims, preferred_element_type=jnp.float32
             )
+            by_imag += lax.dot_general(
+                a, source[1, rows, cols], dims, preferred_element_type=jnp.float32
+            )
+        real = (by_real[:half] - by_imag[half:]).reshape(cs, bins, width)
+        imag = (by_real[half:] + by_imag[:half]).reshape(cs, bins, width)
+        fr = turn[0, :, rows][None]
+        fi = turn[1, :, rows][None]
+        amp[g + 1, k, shard, 0:half, rows] = (
+            (real * fr - imag * fi).reshape(half, width).astype(jnp.bfloat16)
+        )
+        amp[g + 1, k, shard, half:2 * half, rows] = (
+            (real * fi + imag * fr).reshape(half, width).astype(jnp.bfloat16)
+        )
+
+    for d in range(n - 2):
+        forward(jnp.int32(0), d)
 
     @pl.loop(0, phases)
     def _(p):
@@ -244,23 +261,33 @@
                 def _(q):
                     lend(q).start()
 
+        if n > 2:
+            forward(p + 1, 0)
+
         for d in range(n - 1):
             for sign in (lead, -lead):
-                @pl.when(jnp.logical_and(active, inside(me - sign * (d + 1))))
+                @pl.when(
+                    jnp.logical_and(
+                        jnp.logical_and(active, inside(me - sign * (d + 1))),
+                        jnp.logical_not(wanted(g, me + sign)),
+                    )
+                )
                 def _(sign=sign, d=d):
                     arrival(g, k, sign, d).wait_recv()
-                    if d + 1 < n - 1:
-                        @pl.when(wanted(g, me + sign))
-                        def _():
-                            hop(g, k, sign, d + 1).start()
 
         @pl.when(jnp.logical_and(position == 0, active))
         def _():
             load(g).wait()
 
-        @pl.when(active)
-        def _():
-            couple(matrix.at[g], factor.at[g], g, k, me)
+        for tile in range(tiles):
+            @pl.when(active)
+            def _(tile=tile):
+                couple(matrix.at[g], factor.at[g], g, k, me, tile)
+
+            if tile + 1 < n - 2:
+                forward(p + 1, tile + 1)
+        for d in range(tiles + 1, n - 2):
+            forward(p + 1, d)
 
         @pl.when(g < last)
         def _():
@@ -281,7 +308,8 @@
                     def _(q):
                         lend(q).wait_recv()
 
-                couple(lent, lent_factor, last, k, partner)
+                for tile in range(tiles):
+                    couple(lent, lent_factor, last, k, partner, tile)
 
                 @pl.when(k != me)
                 def _():

time: 238 us -> 220 us (0.924)
  Pallas kernels: 229 us -> 210 us
    pallas_call x1, Pallas kernels: 229 us -> 210 us  [shards(): pl.pallas_call(functools.partial(propagate, n, nf, all_bins // 16), out_s...]
where the time goes in v3:
time: 220 us
  Pallas kernels  210 us (95%)
  matrix products  5.51 us (3%)
  local copies, waits for them, and re-layouts  4.01 us (2%)
    pallas_call x1, Pallas kernels, shards(): pl.pallas_call(functools.partial(propagate, n, nf, all_bins // 16), out_s...  210 us
    dot_general x1, matrix products, shards(): lax.dot_general(left, table, (((2,), (0,)), ((), ())), preferred_element_...  5.51 us

profile of v3, /device:TPU:17, one launch (start us, length us, event | category | flops | bytes accessed | tf_op | source)
XLA Modules:
  0.0 220.0 jit_solution(1702597012031973743)
XLA Ops:
  0.0 1.3 copy.12.counts
  1.3 0.8 copy.11
  2.1 0.6 tile.4
  2.7 210.5 %propagate.1 = (bf16[512,4096]{1,0:T(8,128)(2,1)}, bf16[8,2,64,128]{3,2,1,0:T(8,128)(2,1)}) custom-call(bf16[16,2,32,512]{3,2,1,0:T(8,128)(2,1)} %exc.1, bf16[3,1,2,512,2048]{4,3,2,1,0:T(8,128)(2,1)} %coupling.1, f32[32,512]{1,0:T(8,128)} %wavenumber.1, s32[32,1]{1,0:T(8,128)} %copy.12.counts, s32[3]{0:T(128)} %steps.1, bf16[1,2048,512]{2,1,0:T(8,128)(2,1)} %shapes.1, ...), custom_call_target="tpu_custom_call" | custom-call | tf_op jit(solution)/shard_map/propagate/pallas_call | solution.py:423
  213.2 1.2 copy.13
  214.4 0.1 copy.14
  214.5 5.5 %convolution_multiply_fusion = f32[4,64,4096]{2,1,0:T(8,128)} fusion(bf16[4,64,512]{1,2,0:T(8,128)(2,1)S(1)} %bitcast.11, bf16[512,4096]{1,0:T(8,128)(2,1)} %get-tuple-element.8), kind=kOutput, calls=%fused_computation | convolution fusion | flops 1074790400 | bytes 8650752 | tf_op jit(solution)/shard_map/dot_general | solution.py:463

commit v4 on v3

--- a/solution.py
+++ b/solution.py
@@ -13,14 +13,19 @@
 
 
 def phase_order(segments, n):
-    pairs = [(g, position) for g in range(segments) for position in range(n)]
-    return sorted(pairs, key=lambda pair: (pair[1] + pair[0] * 0.625 * n, pair[0]))
+    def key(pair):
+        g, position = pair
+        if segments == 3:
+            return ((0.0, 0.55, 0.9)[g] * n + (1.0, 0.6, 0.25)[g] * position, g)
+        return (position + g * 0.625 * n, g)
+
+    return sorted([(g, position) for g in range(segments) for position in range(n)], key=key)
 
 
 def propagate(
-    n, nf, offset_bin, exc, coupling, wavenumber, counts, steps, shapes, weights,
+    n, nf, offset_bin, exc, coupling, wavenumber, counts, steps, shapes, spectrum,
     table, received,
-    matrix, amp, factor, weighted, landed, lent, lent_factor,
+    matrix, amp, factor, weighted, landed, lent, lent_factor, part, mine, total,
     load_sem, send_sem, recv_sem, own_send, own_recv, out_send, out_recv,
     lend_send, lend_recv, lend_factor_sem,
 ):
@@ -124,12 +129,12 @@
             def _(sign=sign):
                 hop(g, k, sign, 0).start()
 
-    def to_owner(k, shard, which):
+    def to_owner(k):
         return pltpu.make_async_remote_copy(
-            src_ref=amp.at[segments, k, shard],
-            dst_ref=amp.at[segments, k, shard],
-            send_sem=own_send.at[k, which],
-            recv_sem=own_recv.at[shard],
+            src_ref=part.at[0, k],
+            dst_ref=part.at[1, me],
+            send_sem=own_send.at[k],
+            recv_sem=own_recv.at[me],
             device_id={"mode": k},
             device_id_type=pl.DeviceIdType.MESH,
         )
@@ -154,7 +159,11 @@
         )
 
     mode_number = me * modes + lax.broadcasted_iota(jnp.int32, (bins, modes), 1)
-    living = jnp.where(mode_number < counts[...], 1.0, 0.0).astype(jnp.float32)
+    row_number = lax.broadcasted_iota(jnp.int32, (bins, modes), 0)
+    count = jnp.zeros((bins, modes), jnp.int32)
+    for f in range(bins):
+        count = jnp.where(row_number == f, counts[f], count)
+    living = jnp.where(mode_number < count, 1.0, 0.0).astype(jnp.float32)
 
     @pl.loop(0, n)
     def _(k):
@@ -169,15 +178,10 @@
     if n > 1:
         send_own(0, owner(jnp.int32(1)))
 
-    for g in range(segments):
+    def turn_by(g):
         angle = wavenumber[...] * steps[g].astype(jnp.float32)
         factor[g, 0] = living * jnp.cos(angle)
         factor[g, 1] = living * jnp.sin(angle)
-
-    @pl.when(edge)
-    def _():
-        lend_factor().start()
-        load(last).wait()
 
     def table_block(j):
         f = j * bins + offset_bin + lax.broadcasted_iota(jnp.int32, (bins, LANES), 0)
@@ -240,7 +244,18 @@
             (real * fi + imag * fr).reshape(half, width).astype(jnp.bfloat16)
         )
 
-    for d in range(n - 2):
+    turn_by(0)
+    if n > 2:
+        forward(jnp.int32(0), 0)
+    for g in range(1, segments):
+        turn_by(g)
+
+    @pl.when(edge)
+    def _():
+        lend_factor().start()
+        load(last).wait()
+
+    for d in range(1, n - 2):
         forward(jnp.int32(0), d)
 
     @pl.loop(0, phases)
@@ -293,10 +308,6 @@
         def _():
             send_own(g + 1, k)
 
-        @pl.when(jnp.logical_and(jnp.logical_and(g == last, active), k != me))
-        def _():
-            to_owner(k, me, 0).start()
-
         if relieve:
             @pl.when(helping)
             def _():
@@ -311,43 +322,67 @@
                 for tile in range(tiles):
                     couple(lent, lent_factor, last, k, partner, tile)
 
-                @pl.when(k != me)
+        def field_of(shard):
+            rows = pl.ds(pl.multiple_of(shard * modes, modes), modes)
+            return jnp.dot(
+                amp[segments, k, shard], shapes[0, rows, :],
+                preferred_element_type=jnp.float32,
+            )
+
+        @pl.when(jnp.logical_and(g == last, active))
+        def _():
+            mine[...] = field_of(me)
+
+            if relieve:
+                @pl.when(helper)
                 def _():
-                    to_owner(k, partner, 1).start()
+                    mine[...] += field_of(partner)
+
+            @pl.when(k != me)
+            def _():
+                part[0, k] = mine[...].astype(jnp.bfloat16)
+                to_owner(k).start()
+
+            @pl.when(k == me)
+            def _():
+                total[...] = mine[...]
 
         @pl.loop(0, (nf - p + phases - 1) // phases)
         def _(i):
             table_block(p + i * phases)
 
-    @pl.loop(0, n)
-    def _(z):
-        here = jnp.logical_or(
-            jnp.logical_and(z == me, jnp.logical_not(edge)),
-            jnp.logical_and(helper, z == partner),
-        )
-
-        @pl.when(jnp.logical_not(here))
-        def _():
-            sender = jnp.where(at_end(z), jnp.where(z == 0, 1, n - 2), z)
+    @pl.when(edge)
+    def _():
+        total[...] = jnp.zeros_like(total)
+
+    @pl.loop(1, n)
+    def _(i):
+        z = lax.rem(me + i, n)
+
+        @pl.when(jnp.logical_not(at_end(z)))
+        def _():
             pltpu.make_async_remote_copy(
-                src_ref=amp.at[segments, me, z],
-                dst_ref=amp.at[segments, me, z],
-                send_sem=own_send.at[me, 0],
+                src_ref=part.at[0, z],
+                dst_ref=part.at[1, z],
+                send_sem=own_send.at[z],
                 recv_sem=own_recv.at[z],
-                device_id={"mode": sender},
+                device_id={"mode": z},
                 device_id_type=pl.DeviceIdType.MESH,
             ).wait_recv()
-
-    field = jnp.zeros((2 * half, receivers), jnp.float32)
-    for z in range(n):
-        field += jnp.dot(
-            amp[segments, me, z], shapes[0, z * modes:(z + 1) * modes, :],
-            preferred_element_type=jnp.float32,
-        )
-    wr, wi = weights[:, 0:1], weights[:, 1:2]
-    fr, fi = field[:half], field[half:]
-    weighted[0] = (wr * fr - wi * fi).T.astype(jnp.bfloat16)
-    weighted[1] = (wr * fi + wi * fr).T.astype(jnp.bfloat16)
+            total[...] += part[1, z].astype(jnp.float32)
+
+    def weight(c):
+        row = lax.broadcasted_iota(jnp.int32, (bins, receivers), 0)
+        value = jnp.zeros((bins, receivers), jnp.float32)
+        for f in range(bins):
+            value = jnp.where(row == f, spectrum[c, f], value)
+        return value[None]
+
+    wr, wi = weight(0), weight(1)
+    fr = total[0:half].reshape(cs, bins, receivers)
+    fi = total[half:2 * half].reshape(cs, bins, receivers)
+    weighted[0] = (wr * fr - wi * fi).reshape(half, receivers).T.astype(jnp.bfloat16)
+    weighted[1] = (wr * fi + wi * fr).reshape(half, receivers).T.astype(jnp.bfloat16)
 
     def to_receiver(j, slot):
         return pltpu.make_async_remote_copy(
@@ -391,12 +426,7 @@
 
         @pl.when(jnp.logical_not(edge))
         def _():
-            to_owner(k, me, 0).wait_send()
-
-        if relieve:
-            @pl.when(helper)
-            def _():
-                to_owner(k, partner, 1).wait_send()
+            to_owner(k).wait_send()
 
     if relieve:
         @pl.when(edge)
@@ -419,6 +449,7 @@
     rh = receivers // nf
     all_bins = bins * nf
     vmem = pl.BlockSpec(memory_space=pltpu.VMEM)
+    smem = pl.BlockSpec(memory_space=pltpu.SMEM)
     dma = pltpu.SemaphoreType.DMA
     table, received = pl.pallas_call(
         functools.partial(propagate, n, nf, all_bins // 16),
@@ -427,8 +458,7 @@
             jax.ShapeDtypeStruct((nf, 2, rh, half), jnp.bfloat16),
         ),
         in_specs=[
-            vmem, pl.BlockSpec(memory_space=pl.ANY), vmem, vmem,
-            pl.BlockSpec(memory_space=pltpu.SMEM), vmem, vmem,
+            vmem, pl.BlockSpec(memory_space=pl.ANY), vmem, smem, smem, vmem, smem,
         ],
         out_specs=(vmem, vmem),
         scratch_shapes=[
@@ -439,10 +469,13 @@
             pltpu.VMEM((nf, 2, rh, half), jnp.bfloat16),
             pltpu.VMEM((2, modes, all_modes), jnp.bfloat16),
             pltpu.VMEM((2, bins, modes), jnp.float32),
+            pltpu.VMEM((2, n, 2 * half, receivers), jnp.bfloat16),
+            pltpu.VMEM((2 * half, receivers), jnp.float32),
+            pltpu.VMEM((2 * half, receivers), jnp.float32),
             dma((segments,)),
             dma((segments, n, 2, n - 1)),
             dma((segments, n, 2, n - 1)),
-            dma((n, 2)),
+            dma((n,)),
             dma((n,)),
             dma((nf,)),
             dma((nf,)),
@@ -455,8 +488,7 @@
         ),
         name="propagate",
     )(
-        excitation, coupling, wavenumber, mode_counts.reshape(bins, 1), seg_steps, shapes,
-        jnp.tile(spectrum.T, (cs, 1)),
+        excitation, coupling, wavenumber, mode_counts, seg_steps, shapes, spectrum,
     )
     left = received.reshape(nf, 2, rh, cs, bins).transpose(3, 2, 0, 1, 4)
     left = left.reshape(cs, rh, nf * 2 * bins)

time: 220 us -> 216 us (0.982)
  local copies, waits for them, and re-layouts: 4.01 us -> 1.28 us
where the time goes in v4:
time: 216 us
  Pallas kernels  209 us (97%)
  matrix products  5.51 us (3%)
    pallas_call x1, Pallas kernels, shards(): pl.pallas_call(functools.partial(propagate, n, nf, all_bins // 16), out_s...  209 us
    dot_general x1, matrix products, shards(): lax.dot_general(left, table, (((2,), (0,)), ((), ())), preferred_element_...  5.51 us

profile of v4, /device:TPU:17, one launch (start us, length us, event | category | flops | bytes accessed | tf_op | source)
XLA Modules:
  0.0 216.1 jit_solution(7276517345060876875)
XLA Ops:
  0.0 209.3 %propagate.1 = (bf16[512,4096]{1,0:T(8,128)(2,1)}, bf16[8,2,64,128]{3,2,1,0:T(8,128)(2,1)}) custom-call(bf16[16,2,32,512]{3,2,1,0:T(8,128)(2,1)} %exc.1, bf16[3,1,2,512,2048]{4,3,2,1,0:T(8,128)(2,1)} %coupling.1, f32[32,512]{1,0:T(8,128)} %wavenumber.1, s32[32]{0:T(128)} %counts.1, s32[3]{0:T(128)} %steps.1, bf16[1,2048,512]{2,1,0:T(8,128)(2,1)} %shapes.1, ...), custom_call_target="tpu_custom_call" | custom-call | tf_op jit(solution)/shard_map/propagate/pallas_call | solution.py:454
  209.3 1.2 copy.9
  210.5 0.1 copy.10
  210.6 5.5 %convolution_multiply_fusion = f32[4,64,4096]{2,1,0:T(8,128)} fusion(bf16[4,64,512]{1,2,0:T(8,128)(2,1)S(1)} %bitcast.8, bf16[512,4096]{1,0:T(8,128)(2,1)} %get-tuple-element.8), kind=kOutput, calls=%fused_computation | convolution fusion | flops 1074790400 | bytes 8650752 | tf_op jit(solution)/shard_map/dot_general | solution.py:495

commit v5 on v4

--- a/solution.py
+++ b/solution.py
@@ -25,7 +25,7 @@
 def propagate(
     n, nf, offset_bin, exc, coupling, wavenumber, counts, steps, shapes, spectrum,
     table, received,
-    matrix, amp, factor, weighted, landed, lent, lent_factor, part, mine, total,
+    matrix, amp, factor, weighted, landed, lent, lent_narrow, narrow, lent_factor, part, mine, total,
     load_sem, send_sem, recv_sem, own_send, own_recv, out_send, out_recv,
     lend_send, lend_recv, lend_factor_sem,
 ):
@@ -80,8 +80,8 @@
 
     def lend_factor():
         return pltpu.make_async_remote_copy(
-            src_ref=factor.at[last],
-            dst_ref=lent_factor,
+            src_ref=narrow,
+            dst_ref=lent_narrow,
             send_sem=lend_factor_sem.at[0],
             recv_sem=lend_factor_sem.at[1],
             device_id={"mode": inward},
@@ -169,8 +169,8 @@
     def _(k):
         for c in range(2):
             x = exc[pl.ds(k * cs, cs), c].astype(jnp.float32) * living[None]
-            amp[0, k, me, c * half:(c + 1) * half, :] = (
-                x.reshape(half, modes).astype(jnp.bfloat16)
+            amp[0, k, me, :, c * half:(c + 1) * half] = (
+                x.reshape(half, modes).T.astype(jnp.bfloat16)
             )
 
     pl.semaphore_wait(barrier, n - 1 + nf - 1)
@@ -178,10 +178,15 @@
     if n > 1:
         send_own(0, owner(jnp.int32(1)))
 
+    def widen(x):
+        return jnp.broadcast_to(x[None], (cs, bins, modes)).reshape(half, modes).T
+
     def turn_by(g):
         angle = wavenumber[...] * steps[g].astype(jnp.float32)
-        factor[g, 0] = living * jnp.cos(angle)
-        factor[g, 1] = living * jnp.sin(angle)
+        narrow[0] = living * jnp.cos(angle)
+        narrow[1] = living * jnp.sin(angle)
+        for c in range(2):
+            factor[g, c] = widen(narrow[c])
 
     def table_block(j):
         f = j * bins + offset_bin + lax.broadcasted_iota(jnp.int32, (bins, LANES), 0)
@@ -221,28 +226,15 @@
 
     def couple(source, turn, g, k, shard, tile):
         rows = slice(tile * width, (tile + 1) * width)
-        by_real = jnp.zeros((2 * half, width), jnp.float32)
-        by_imag = jnp.zeros((2 * half, width), jnp.float32)
-        for z in range(n):
-            a = amp[g, k, z]
-            cols = slice(z * modes, (z + 1) * modes)
-            dims = (((1,), (1,)), ((), ()))
-            by_real += lax.dot_general(
-                a, source[0, rows, cols], dims, preferred_element_type=jnp.float32
-            )
-            by_imag += lax.dot_general(
-                a, source[1, rows, cols], dims, preferred_element_type=jnp.float32
-            )
-        real = (by_real[:half] - by_imag[half:]).reshape(cs, bins, width)
-        imag = (by_real[half:] + by_imag[:half]).reshape(cs, bins, width)
-        fr = turn[0, :, rows][None]
-        fi = turn[1, :, rows][None]
-        amp[g + 1, k, shard, 0:half, rows] = (
-            (real * fr - imag * fi).reshape(half, width).astype(jnp.bfloat16)
-        )
-        amp[g + 1, k, shard, half:2 * half, rows] = (
-            (real * fi + imag * fr).reshape(half, width).astype(jnp.bfloat16)
-        )
+        a = amp[g, k].reshape(n * modes, 2 * half)
+        c = source[:, rows, :].reshape(2 * width, n * modes)
+        product = jnp.dot(c, a, preferred_element_type=jnp.float32)
+        by_real, by_imag = product[:width], product[width:]
+        real = by_real[:, :half] - by_imag[:, half:]
+        imag = by_real[:, half:] + by_imag[:, :half]
+        fr, fi = turn[0, rows], turn[1, rows]
+        amp[g + 1, k, shard, rows, 0:half] = (real * fr - imag * fi).astype(jnp.bfloat16)
+        amp[g + 1, k, shard, rows, half:2 * half] = (real * fi + imag * fr).astype(jnp.bfloat16)
 
     turn_by(0)
     if n > 2:
@@ -314,6 +306,8 @@
                 @pl.when(position == 0)
                 def _():
                     lend_factor().wait_recv()
+                    for c in range(2):
+                        lent_factor[c] = widen(lent_narrow[c])
 
                     @pl.loop(0, pieces)
                     def _(q):
@@ -324,8 +318,8 @@
 
         def field_of(shard):
             rows = pl.ds(pl.multiple_of(shard * modes, modes), modes)
-            return jnp.dot(
-                amp[segments, k, shard], shapes[0, rows, :],
+            return lax.dot_general(
+                shapes[0, rows, :], amp[segments, k, shard], (((0,), (0,)), ((), ())),
                 preferred_element_type=jnp.float32,
             )
 
@@ -372,17 +366,16 @@
             total[...] += part[1, z].astype(jnp.float32)
 
     def weight(c):
-        row = lax.broadcasted_iota(jnp.int32, (bins, receivers), 0)
-        value = jnp.zeros((bins, receivers), jnp.float32)
+        f_number = lax.rem(lax.broadcasted_iota(jnp.int32, (8, half), 1), bins)
+        value = jnp.zeros((8, half), jnp.float32)
         for f in range(bins):
-            value = jnp.where(row == f, spectrum[c, f], value)
-        return value[None]
+            value = jnp.where(f_number == f, spectrum[c, f], value)
+        return value[0:1]
 
     wr, wi = weight(0), weight(1)
-    fr = total[0:half].reshape(cs, bins, receivers)
-    fi = total[half:2 * half].reshape(cs, bins, receivers)
-    weighted[0] = (wr * fr - wi * fi).reshape(half, receivers).T.astype(jnp.bfloat16)
-    weighted[1] = (wr * fi + wi * fr).reshape(half, receivers).T.astype(jnp.bfloat16)
+    fr, fi = total[:, 0:half], total[:, half:2 * half]
+    weighted[0] = (wr * fr - wi * fi).astype(jnp.bfloat16)
+    weighted[1] = (wr * fi + wi * fr).astype(jnp.bfloat16)
 
     def to_receiver(j, slot):
         return pltpu.make_async_remote_copy(
@@ -463,15 +456,17 @@
         out_specs=(vmem, vmem),
         scratch_shapes=[
             pltpu.VMEM((segments, 2, modes, all_modes), jnp.bfloat16),
-            pltpu.VMEM((segments + 1, n, n, 2 * half, modes), jnp.bfloat16),
-            pltpu.VMEM((segments, 2, bins, modes), jnp.float32),
+            pltpu.VMEM((segments + 1, n, n, modes, 2 * half), jnp.bfloat16),
+            pltpu.VMEM((segments, 2, modes, half), jnp.float32),
             pltpu.VMEM((2, receivers, half), jnp.bfloat16),
             pltpu.VMEM((nf, 2, rh, half), jnp.bfloat16),
             pltpu.VMEM((2, modes, all_modes), jnp.bfloat16),
             pltpu.VMEM((2, bins, modes), jnp.float32),
-            pltpu.VMEM((2, n, 2 * half, receivers), jnp.bfloat16),
-            pltpu.VMEM((2 * half, receivers), jnp.float32),
-            pltpu.VMEM((2 * half, receivers), jnp.float32),
+            pltpu.VMEM((2, bins, modes), jnp.float32),
+            pltpu.VMEM((2, modes, half), jnp.float32),
+            pltpu.VMEM((2, n, receivers, 2 * half), jnp.bfloat16),
+            pltpu.VMEM((receivers, 2 * half), jnp.float32),
+            pltpu.VMEM((receivers, 2 * half), jnp.float32),
             dma((segments,)),
             dma((segments, n, 2, n - 1)),
             dma((segments, n, 2, n - 1)),

time: 216 us -> 217 us (level)
  no operation moved by 1% of the time
where the time goes in v5:
time: 217 us
  Pallas kernels  210 us (97%)
  matrix products  5.51 us (3%)
    pallas_call x1, Pallas kernels, shards(): pl.pallas_call(functools.partial(propagate, n, nf, all_bins // 16), out_s...  210 us
    dot_general x1, matrix products, shards(): lax.dot_general(left, table, (((2,), (0,)), ((), ())), preferred_element_...  5.51 us

profile of v5, /device:TPU:17, one launch (start us, length us, event | category | flops | bytes accessed | tf_op | source)
XLA Modules:
  0.0 216.6 jit_solution(15570766305864238220)
XLA Ops:
  0.0 209.8 %propagate.1 = (bf16[512,4096]{1,0:T(8,128)(2,1)}, bf16[8,2,64,128]{3,2,1,0:T(8,128)(2,1)}) custom-call(bf16[16,2,32,512]{3,2,1,0:T(8,128)(2,1)} %exc.1, bf16[3,1,2,512,2048]{4,3,2,1,0:T(8,128)(2,1)} %coupling.1, f32[32,512]{1,0:T(8,128)} %wavenumber.1, s32[32]{0:T(128)} %counts.1, s32[3]{0:T(128)} %steps.1, bf16[1,2048,512]{2,1,0:T(8,128)(2,1)} %shapes.1, ...), custom_call_target="tpu_custom_call" | custom-call | tf_op jit(solution)/shard_map/propagate/pallas_call | solution.py:447
  209.8 1.2 copy.9
  211.0 0.1 copy.10
  211.1 5.5 %convolution_multiply_fusion = f32[4,64,4096]{2,1,0:T(8,128)} fusion(bf16[4,64,512]{1,2,0:T(8,128)(2,1)S(1)} %bitcast.8, bf16[512,4096]{1,0:T(8,128)(2,1)} %get-tuple-element.8), kind=kOutput, calls=%fused_computation | convolution fusion | flops 1074790400 | bytes 8650752 | tf_op jit(solution)/shard_map/dot_general | solution.py:490

commit v6 on v5

--- a/solution.py
+++ b/solution.py
@@ -15,8 +15,6 @@
 def phase_order(segments, n):
     def key(pair):
         g, position = pair
-        if segments == 3:
-            return ((0.0, 0.55, 0.9)[g] * n + (1.0, 0.6, 0.25)[g] * position, g)
         return (position + g * 0.625 * n, g)
 
     return sorted([(g, position) for g in range(segments) for position in range(n)], key=key)
@@ -249,6 +247,8 @@
 
     for d in range(1, n - 2):
         forward(jnp.int32(0), d)
+    if n > 2:
+        forward(jnp.int32(1), 0)
 
     @pl.loop(0, phases)
     def _(p):
@@ -269,7 +269,9 @@
                     lend(q).start()
 
         if n > 2:
-            forward(p + 1, 0)
+            forward(p + 2, 0)
+        if n > 3:
+            forward(p + 1, 1)
 
         for d in range(n - 1):
             for sign in (lead, -lead):
@@ -291,9 +293,9 @@
             def _(tile=tile):
                 couple(matrix.at[g], factor.at[g], g, k, me, tile)
 
-            if tile + 1 < n - 2:
-                forward(p + 1, tile + 1)
-        for d in range(tiles + 1, n - 2):
+            if tile + 2 < n - 2:
+                forward(p + 1, tile + 2)
+        for d in range(tiles + 2, n - 2):
             forward(p + 1, d)
 
         @pl.when(g < last)

time: 217 us -> 214 us (0.986)
  Pallas kernels: 210 us -> 207 us
    pallas_call x1, Pallas kernels: 210 us -> 207 us  [shards(): pl.pallas_call(functools.partial(propagate, n, nf, all_bins // 16), out_s...]
where the time goes in v6:
time: 214 us; the launch traced here: 213 us
  Pallas kernels  207 us (97%)
  matrix products  5.51 us (3%)
    pallas_call x1, Pallas kernels, shards(): pl.pallas_call(functools.partial(propagate, n, nf, all_bins // 16), out_s...  207 us
    dot_general x1, matrix products, shards(): lax.dot_general(left, table, (((2,), (0,)), ((), ())), preferred_element_...  5.51 us

profile of v6, /device:TPU:17, one launch (start us, length us, event | category | flops | bytes accessed | tf_op | source)
XLA Modules:
  0.0 213.4 jit_solution(17203429153112843271)
XLA Ops:
  0.0 206.6 %propagate.1 = (bf16[512,4096]{1,0:T(8,128)(2,1)}, bf16[8,2,64,128]{3,2,1,0:T(8,128)(2,1)}) custom-call(bf16[16,2,32,512]{3,2,1,0:T(8,128)(2,1)} %exc.1, bf16[3,1,2,512,2048]{4,3,2,1,0:T(8,128)(2,1)} %coupling.1, f32[32,512]{1,0:T(8,128)} %wavenumber.1, s32[32]{0:T(128)} %counts.1, s32[3]{0:T(128)} %steps.1, bf16[1,2048,512]{2,1,0:T(8,128)(2,1)} %shapes.1, ...), custom_call_target="tpu_custom_call" | custom-call | tf_op jit(solution)/shard_map/propagate/pallas_call | solution.py:449
  206.6 1.2 copy.9
  207.8 0.1 copy.10
  207.9 5.5 %convolution_multiply_fusion = f32[4,64,4096]{2,1,0:T(8,128)} fusion(bf16[4,64,512]{1,2,0:T(8,128)(2,1)S(1)} %bitcast.8, bf16[512,4096]{1,0:T(8,128)(2,1)} %get-tuple-element.8), kind=kOutput, calls=%fused_computation | convolution fusion | flops 1074790400 | bytes 8650752 | tf_op jit(solution)/shard_map/dot_general | solution.py:492
